TPU v7x, 256 devices: a whole 4x4x8 slice. The times are simulated.
256 devices in a mesh: replica: 4 (over y), shard: 64 (over z, x, core).
Axes of the slice: x: 4, y: 4, z: 8, core: 2. Of those that a mesh axis runs over, the one named last changes fastest.
Arguments:
- grads: bfloat16 [4, 32, 512, 3584], P('replica', None, 'shard')
- owner_table: int32 [4, 64], replicated, may hold values from 0 to 63, each once within a row
- momentum: float32 [4, 64, 512, 512], P('replica', 'shard'), may hold values from -6 to 6
- second: float32 [4, 64, 512, 512], P('replica', 'shard'), may hold values from 0.01 to 1
- left_stat: float32 [4, 64, 512, 512], P('replica', 'shard')
- right_stat: float32 [4, 64, 512, 512], P('replica', 'shard')
- left_root: float32 [4, 64, 512, 512], P('replica', 'shard')
- right_root: float32 [4, 64, 512, 512], P('replica', 'shard')
Outputs:
- update: bfloat16 [32, 512, 3584], P(None, 'shard', 'replica')
- momentum_out: float32 [4, 64, 512, 512], P('replica', 'shard')
- second_out: float32 [4, 64, 512, 512], P('replica', 'shard')
- left_out: float32 [4, 64, 512, 512], P('replica', 'shard')
- right_out: float32 [4, 64, 512, 512], P('replica', 'shard')
Inputs may be any that keep to these rules, and one draw needn't show every extreme that they name: Each row of owner_table names every device index 0 to 63 once.
All inputs are finite; a program needn't handle non-finite values.
Results may differ from a plain program's by a relative error of at most 0.014.
Values may be sent and summed in bfloat16 or wider, within the bound.
A program may use at most 64 MiB of HBM per device.

v0:
```python
import jax
import jax.numpy as jnp
from jax import lax
from jax.sharding import PartitionSpec as P

BETA_STAT = 0.95
BETA_SECOND = 0.99
BETA_MOMENT = 0.9
EPS_ADAM = 1e-08
EPS_NORM = 1e-06
LEARN_RATE = 0.5
HIGHEST = lax.Precision.HIGHEST


def per_device(grads, owner_table, momentum, second, left_stat, right_stat, left_root, right_root):
    shards = lax.axis_size("shard")
    groups = lax.axis_size("replica")
    replica_index = lax.axis_index("replica")
    owner_index = lax.axis_index("shard")
    row_blocks = grads.shape[1]
    rows_dev = grads.shape[2]
    full_width = grads.shape[3]
    block_size = left_stat.shape[2]
    quarter = full_width // groups
    col_blocks = (quarter + block_size - 1) // block_size
    nblocks = row_blocks * col_blocks
    owner_ids = jnp.arange(shards, dtype=jnp.int32)
    block_ids = jnp.arange(nblocks, dtype=jnp.int32)
    row_ids = jnp.arange(rows_dev, dtype=jnp.int32)
    matches = owner_table[:, None, :] == owner_ids[None, :, None]
    inverse = jnp.sum(jnp.where(matches, block_ids[None, None, :], 0), axis=2)
    own_table = lax.dynamic_index_in_dim(owner_table, replica_index, 0, keepdims=False)
    own_inverse = lax.dynamic_index_in_dim(inverse, replica_index, 0, keepdims=False)
    own_block = lax.dynamic_index_in_dim(own_inverse, owner_index, 0, keepdims=False)
    pad_cols = col_blocks * block_size - quarter
    summed = lax.psum_scatter(
        grads[0].astype(jnp.float32).astype(jnp.bfloat16),
        "replica",
        scatter_dimension=2,
        tiled=True,
    ).astype(jnp.float32)
    padded = jnp.pad(summed, ((0, 0), (0, 0), (0, pad_cols)))
    pieces = padded.reshape(row_blocks, rows_dev, col_blocks, block_size)
    row_pick = (own_inverse // col_blocks)[:, None]
    col_pick = (own_inverse % col_blocks)[:, None]
    outgoing = pieces[row_pick, row_ids[None, :], col_pick, :]
    arrived = lax.all_to_all(outgoing, "shard", split_axis=0, concat_axis=0, tiled=True)
    grad_block = arrived.reshape(block_size, block_size)
    columns = own_block % col_blocks * block_size + jnp.arange(block_size, dtype=jnp.int32)
    col_mask = (columns < quarter).astype(jnp.float32)[None, :]
    gram_left = jnp.dot(grad_block, grad_block.T, precision=HIGHEST)
    gram_right = jnp.dot(grad_block.T, grad_block, precision=HIGHEST)
    left_new = BETA_STAT * left_stat[0, 0] + (1.0 - BETA_STAT) * gram_left
    right_new = BETA_STAT * right_stat[0, 0] + (1.0 - BETA_STAT) * gram_right
    second_new = BETA_SECOND * second[0, 0] + (1.0 - BETA_SECOND) * grad_block * grad_block
    adam_dir = col_mask * grad_block / (jnp.sqrt(second_new) + EPS_ADAM)
    shaped = (
        jnp.dot(
            jnp.dot(left_root[0, 0], grad_block, precision=HIGHEST),
            right_root[0, 0],
            precision=HIGHEST,
        )
        * col_mask
    )
    graft_scale = jnp.sqrt(jnp.sum(adam_dir * adam_dir) + EPS_NORM) / jnp.sqrt(
        jnp.sum(shaped * shaped) + EPS_NORM
    )
    moment_new = BETA_MOMENT * momentum[0, 0] + graft_scale * shaped
    step_block = (-LEARN_RATE * moment_new).astype(jnp.bfloat16)
    returned = lax.all_to_all(
        step_block.reshape(shards, rows_dev, block_size),
        "shard",
        split_axis=0,
        concat_axis=0,
        tiled=True,
    )
    table_grid = own_table.reshape(row_blocks, col_blocks)[:, None, :]
    placed = returned[table_grid, row_ids[None, :, None], :]
    update = placed.reshape(row_blocks, rows_dev, col_blocks * block_size)[:, :, :quarter]
    shape_own = (1, 1, block_size, block_size)
    return (
        update,
        moment_new.reshape(shape_own),
        second_new.reshape(shape_own),
        left_new.reshape(shape_own),
        right_new.reshape(shape_own),
    )


def solution(mesh):
    return jax.shard_map(
        per_device,
        mesh=mesh,
        in_specs=(
            P("replica", None, "shard", None),
            P(),
            P("replica", "shard", None, None),
            P("replica", "shard", None, None),
            P("replica", "shard", None, None),
            P("replica", "shard", None, None),
            P("replica", "shard", None, None),
            P("replica", "shard", None, None),
        ),
        out_specs=(
            P(None, "shard", "replica"),
            P("replica", "shard", None, None),
            P("replica", "shard", None, None),
            P("replica", "shard", None, None),
            P("replica", "shard", None, None),
        ),
        check_vma=False,
    )
```

profile of v0, /device:TPU:1, one launch (start us, length us, event | category | flops | bytes accessed | tf_op | source)
XLA Modules:
  0.0 220.9 jit_solution(17545836225794034297)
XLA Ops:
  7.2 0.0 copy-start
  7.2 0.0 reduce-scatter.4.cloned.1.call-start
  7.2 24.5 %copy.20 = bf16[32,8,3584]{1,0,2:T(8,128)(2,1)} copy(bf16[32,8,3584]{2,1,0:T(8,128)(2,1)} %bitcast.76) | data formatting | bytes 3670016
  31.8 0.0 copy-start.2
  31.8 41.6 %reshape.196 = bf16[3584,256]{1,0:T(8,128)(2,1)} reshape(bf16[3584,32,8]{2,1,0:T(8,128)(2,1)} %bitcast.73) | data formatting | bytes 3670016
  73.3 0.0 reduce-scatter.4.cloned.1.call-update
  73.4 0.0 copy-done.2
  73.4 0.1 select_reduce_fusion
  73.6 0.1 copy.19
  73.7 0.1 reshape.182
  73.8 33.7 %reduce-scatter.4.cloned.1.call-done = bf16[896,256]{1,0:T(8,128)(2,1)} async-done(((bf16[3584,256]{1,0:T(8,128)(2,1)}), bf16[896,256]{1,0:T(8,128)(2,1)}) %reduce-scatter.4.cloned.1.call-update) | async-done | bytes 458768
  107.5 10.6 %reshape.197 = bf16[896,32,8]{2,1,0:T(8,128)(2,1)} reshape(bf16[896,256]{1,0:T(8,128)(2,1)} %reduce-scatter.4.cloned.1.call-done) | data formatting | bytes 917504
  118.1 8.8 %copy.21 = bf16[32,8,896]{2,1,0:T(8,128)(2,1)S(1)} copy(bf16[32,8,896]{1,0,2:T(8,128)(2,1)} %bitcast.74) | data formatting | bytes 917504
  126.9 0.1 pad_convert_fusion
  127.1 0.9 reshape.181
  128.0 0.0 copy-start.1
  128.0 4.9 %gather_fusion = f32[512,512]{1,0:T(8,128)} fusion(f32[32,8,2,512]{3,2,1,0:T(2,128)S(1)} %reshape.181, s32[512]{0:T(512)S(1)} %reshape.182), kind=kCustom, calls=%fused_computation | custom fusion | bytes 2103296 | tf_op jit(solution)/shard_map/gather | solution.py:46
  132.8 10.6 %all-to-all-start = ((f32[64,8,512]{2,1,0:T(8,128)}), f32[64,8,512]{2,1,0:T(8,128)S(1)}, u32[]{:S(2)}, u32[]{:S(2)}) async-start(f32[64,8,512]{2,1,0:T(8,128)} %bitcast.75), calls=%async_computation | async-start | bytes 2097152 | tf_op jit(solution)/shard_map/all_to_all | solution.py:47
  143.4 0.6 dynamic_slice.11
  146.0 0.1 broadcast_in_dim_reshape.3
  146.1 0.1 reshape.188
  146.3 25.1 %all-to-all-done = f32[64,8,512]{2,1,0:T(8,128)S(1)} async-done(((f32[64,8,512]{2,1,0:T(8,128)}), f32[64,8,512]{2,1,0:T(8,128)S(1)}, u32[]{:S(2)}, u32[]{:S(2)}) %all-to-all-start) | async-done | bytes 1048608 | tf_op jit(solution)/shard_map/all_to_all | solution.py:47
  171.4 4.7 %fusion.12 = f32[512,512]{1,0:T(8,128)S(1)} fusion(f32[1,1,512,512]{3,2,1,0:T(8,128)} %param.14, f32[64,8,512]{2,1,0:T(8,128)S(1)} %all-to-all-done), kind=kOutput, calls=%fused_computation.19 | convolution fusion | flops 1610612736 | bytes 3145728 | tf_op jit(solution)/shard_map/dot_general | solution.py:59
  176.1 0.0 copy-done
  176.1 3.4 %multiply_reduce_fusion = (f32[]{:T(128)}, f32[512,512]{1,0:T(8,128)}) fusion(f32[512]{0:T(512)S(1)} %fusion.21, f32[512,512]{1,0:T(8,128)S(1)} %fusion.12, f32[1,1,512,512]{3,2,1,0:T(8,128)S(1)} %copy-done), kind=kOutput, calls=%fused_computation.25 | convolution fusion | flops 1611399168 | bytes 3147780 | tf_op jit(solution)/shard_map/dot_general | solution.py:58
  180.2 0.0 copy-done.1
  180.2 1.2 fusion.16
  182.1 2.9 %fusion.18 = (f32[1,1,512,512]{3,2,1,0:T(8,128)}, bf16[64,8,512]{2,1,0:T(8,128)(2,1)}) fusion(f32[512,512]{1,0:T(8,128)} %get-tuple-element.10, f32[]{:T(128)S(6)} %div.21, f32[1,1,512,512]{3,2,1,0:T(8,128)} %param.10), kind=kLoop, calls=%fused_computation.29 | loop fusion | flops 1310720 | bytes 3670020 | tf_op jit(solution)/shard_map/reshape | solution.py:83
  185.1 6.5 %all-to-all-start.1 = ((bf16[64,8,512]{2,1,0:T(8,128)(2,1)}), bf16[64,8,512]{2,1,0:T(8,128)(2,1)S(1)}, u32[]{:S(2)}, u32[]{:S(2)}) async-start(bf16[64,8,512]{2,1,0:T(8,128)(2,1)} %get-tuple-element.8), calls=%async_computation.1 | async-start | bytes 1048576 | tf_op jit(solution)/shard_map/all_to_all | solution.py:70
  191.5 2.4 %fusion.10 = f32[1,1,512,512]{3,2,1,0:T(8,128)} fusion(f32[64,8,512]{2,1,0:T(8,128)S(1)} %all-to-all-done, f32[1,1,512,512]{3,2,1,0:T(8,128)} %param.11), kind=kLoop, calls=%fused_computation.17 | loop fusion | flops 1048576 | bytes 3145728 | tf_op jit(solution)/shard_map/add | solution.py:55
  194.0 4.1 %fusion.1 = f32[1,1,512,512]{3,2,1,0:T(8,128)} fusion(f32[64,8,512]{2,1,0:T(8,128)S(1)} %all-to-all-done, f32[1,1,512,512]{3,2,1,0:T(8,128)} %param.12), kind=kOutput, calls=%fused_computation.7 | convolution fusion | flops 1611399168 | bytes 3145728 | tf_op jit(solution)/shard_map/dot_general | solution.py:51
  198.1 4.1 %fusion.4 = f32[1,1,512,512]{3,2,1,0:T(8,128)} fusion(f32[64,8,512]{2,1,0:T(8,128)S(1)} %all-to-all-done, f32[1,1,512,512]{3,2,1,0:T(8,128)} %param.13), kind=kOutput, calls=%fused_computation.11 | convolution fusion | flops 1611399168 | bytes 3145728 | tf_op jit(solution)/shard_map/dot_general | solution.py:52
  202.2 7.1 %all-to-all-done.1 = bf16[64,8,512]{2,1,0:T(8,128)(2,1)S(1)} async-done(((bf16[64,8,512]{2,1,0:T(8,128)(2,1)}), bf16[64,8,512]{2,1,0:T(8,128)(2,1)S(1)}, u32[]{:S(2)}, u32[]{:S(2)}) %all-to-all-start.1) | async-done | bytes 524320 | tf_op jit(solution)/shard_map/all_to_all | solution.py:70
  209.2 3.8 %gather_fusion.1 = bf16[512,512]{1,0:T(8,128)(2,1)S(1)} fusion(bf16[64,8,512]{2,1,0:T(8,128)(2,1)S(1)} %all-to-all-done.1, s32[512]{0:T(512)S(1)} %reshape.188), kind=kCustom, calls=%fused_computation.1 | custom fusion | bytes 1052672 | tf_op jit(solution)/shard_map/gather | solution.py:78
  213.1 0.2 reshape.175
  213.3 0.8 slice.9
  (7 shorter events, 0.1 us)
Async XLA Ops:
  7.2 168.9 %copy-start = (f32[1,1,512,512]{3,2,1,0:T(8,128)S(1)}, f32[1,1,512,512]{3,2,1,0:T(8,128)}, u32[]{:S(2)}) copy-start(f32[1,1,512,512]{3,2,1,0:T(8,128)} %param.15) | copy-start | bytes 3145732
  7.2 100.3 %reduce-scatter.4.cloned.1.call-start = ((), (), s32[]{:S(2)}) async-start(), calls=%async_computation.3 | async-start | bytes 2293760
  31.8 41.6 %copy-start.2 = (s32[4,64]{1,0:T(4,128)S(1)}, s32[4,64]{1,0:T(4,128)}, u32[]{:S(2)}) copy-start(s32[4,64]{1,0:T(4,128)} %param.9) | copy-start | bytes 3076
  128.0 52.3 %copy-start.1 = (f32[1,1,512,512]{3,2,1,0:T(8,128)S(1)}, f32[1,1,512,512]{3,2,1,0:T(8,128)}, u32[]{:S(2)}) copy-start(f32[1,1,512,512]{3,2,1,0:T(8,128)} %param.11) | copy-start | bytes 3145732
  132.8 38.6 %all-to-all-start = ((f32[64,8,512]{2,1,0:T(8,128)}), f32[64,8,512]{2,1,0:T(8,128)S(1)}, u32[]{:S(2)}, u32[]{:S(2)}) async-start(f32[64,8,512]{2,1,0:T(8,128)} %bitcast.75), calls=%async_computation | async-start | bytes 2097152 | tf_op jit(solution)/shard_map/all_to_all | solution.py:47
  185.1 24.2 %all-to-all-start.1 = ((bf16[64,8,512]{2,1,0:T(8,128)(2,1)}), bf16[64,8,512]{2,1,0:T(8,128)(2,1)S(1)}, u32[]{:S(2)}, u32[]{:S(2)}) async-start(bf16[64,8,512]{2,1,0:T(8,128)(2,1)} %get-tuple-element.8), calls=%async_computation.1 | async-start | bytes 1048576 | tf_op jit(solution)/shard_map/all_to_all | solution.py:70
Sparse Core Ops, SparseCore 0:
  73.5 33.9 reduce-scatter.3
where the time goes:
time: 223 us; the launch traced here: 221 us
  local copies, waits for them, and re-layouts  97.1 us (44%)
  waiting for transfers between devices  65.9 us (30%)
  between operations  17.6 us (8%)
  starting transfers between devices  17.1 us (8%)
  matrix products  16.3 us (7%)
  other arithmetic  6.89 us (3%)
    unnamed x10, local copies, waits for them, and re-layouts  85.6 us
    unnamed x2, waiting for transfers between devices  33.8 us
    all_to_all x1, waiting for transfers between devices, per_device(): lax.all_to_all(outgoing, 'shard', split_axis=0, concat_axis=0, tiled=True)  25.1 us
    all_to_all x1, starting transfers between devices, per_device(): lax.all_to_all(outgoing, 'shard', split_axis=0, concat_axis=0, tiled=True)  10.6 us
    all_to_all x1, waiting for transfers between devices, per_device(): lax.all_to_all(step_block.reshape(shards, rows_dev, block_size), 'shard',...  7.09 us
    all_to_all x1, starting transfers between devices, per_device(): lax.all_to_all(step_block.reshape(shards, rows_dev, block_size), 'shard',...  6.47 us
    gather x1, local copies, waits for them, and re-layouts, per_device(): outgoing = pieces[row_pick, row_ids[None, :], col_pick, :]  4.86 us
    dot_general x1, matrix products, per_device(): jnp.dot(left_root[0, 0], grad_block, precision=HIGHEST)  4.69 us
  transfers between devices with their start and end apart: 3, of which 3 were waited for; matrix products, arithmetic and copies ran while one was open for 5% of the time, Pallas kernels for 0%

commit v1 on v0

v1 whole, which is shorter than its diff:
```python
import functools

import jax
import jax.numpy as jnp
from jax import lax
from jax.experimental import pallas as pl
from jax.experimental.pallas import tpu as pltpu
from jax.sharding import PartitionSpec as P

BETA_STAT = 0.95
BETA_SECOND = 0.99
BETA_MOMENT = 0.9
EPS_ADAM = 1e-08
EPS_NORM = 1e-06
LEARN_RATE = 0.5
MESH = pl.DeviceIdType.MESH
F32 = jnp.float32
BF16 = jnp.bfloat16
CHUNKS = 2


def kernel(cfg, inv_ref, tab_ref, g_ref, mom_in, sec_in, ls_in, rs_in, lr_in, rr_in, upd_out, mom_out, sec_out, left_out, right_out, *scratch):
    groups, shards, rb, rows_dev, quarter, block, n, width = cfg
    half = rb // 2
    scratch = list(scratch)

    def take(count):
        got = scratch[:count]
        del scratch[:count]
        return got

    own_p, from_next, from_prev = take(n), take(n), take(n)
    relay = [take(2) for _ in range(n)]
    relay_own = [take(2) for _ in range(n)]
    out_p, arrived = take(n), take(n)
    mom, sec, ls, rs, lr, rr = take(6)
    lroot, rroot, gb, shaped, back, back_arrived, upd = take(7)
    in_sem, own_sem, relay_own_sem, y_send, y_recv, a_send, a_recv, b_send, b_recv, o_sem = take(10)

    r, s = lax.axis_index("replica"), lax.axis_index("shard")
    nxt, prv, opp = lax.rem(r + 1, groups), lax.rem(r + groups - 1, groups), lax.rem(r + 2, groups)

    barrier = pltpu.get_barrier_semaphore()
    for peer in (nxt, prv):
        pl.semaphore_signal(barrier, inc=1, device_id=(peer, s), device_id_type=MESH)

    def greet(k, carry):
        pl.semaphore_signal(barrier, inc=1, device_id=(r, lax.rem(s + k, shards)), device_id_type=MESH)
        return carry

    lax.fori_loop(1, shards, greet, 0)

    def part(j, c):
        start = c * block + j * width
        return start, min(width, quarter - start)

    def piece(q, lo, rows, j, c):
        start, wide = part(j, c)
        return g_ref.at[pl.ds(lo, rows), :, pl.ds(pl.multiple_of(q * quarter + start, 128), wide)]

    parts = [(j, c) for j in range(n) for c in range(2)]
    own_copies = {}
    for j, c in parts:
        wide = part(j, c)[1]
        own_copies[j, c] = [
            pltpu.make_async_copy(piece(prv, 0, half, j, c), relay_own[j][0].at[c, :, :, pl.ds(0, wide)], relay_own_sem.at[j, 0, c]),
            pltpu.make_async_copy(piece(nxt, half, half, j, c), relay_own[j][1].at[c, :, :, pl.ds(0, wide)], relay_own_sem.at[j, 1, c]),
            pltpu.make_async_copy(piece(r, 0, rb, j, c), own_p[j].at[c, :, :, pl.ds(0, wide)], own_sem.at[j, c]),
        ]
        for copy in own_copies[j, c]:
            copy.start()
        if wide < width:
            for buf in (own_p[j], from_next[j], from_prev[j]):
                buf[c, :, :, wide:] = jnp.zeros((rb, rows_dev, width - wide), BF16)
    in_copies = [
        pltpu.make_async_copy(src, dst, in_sem.at[i])
        for i, (src, dst) in enumerate(((lr_in, lr), (rr_in, rr), (sec_in, sec), (mom_in, mom), (ls_in, ls), (rs_in, rs)))
    ]
    for copy in in_copies:
        copy.start()

    def y_copy(kind, way, j, c, src, dst):
        return pltpu.make_async_remote_copy(
            src_ref=src,
            dst_ref=dst,
            send_sem=y_send.at[kind, way, j, c],
            recv_sem=y_recv.at[kind, way, j, c],
            device_id=(nxt if way else prv, s),
            device_id_type=MESH,
        )

    first, direct, onward = {}, {}, {}
    for j, c in parts:
        wide = pl.ds(0, part(j, c)[1])
        lower, upper = pl.ds(0, half), pl.ds(half, half)
        first[j, c] = [
            y_copy(0, 0, j, c, piece(opp, 0, half, j, c), relay[j][0].at[c, :, :, wide]),
            y_copy(0, 1, j, c, piece(opp, half, half, j, c), relay[j][1].at[c, :, :, wide]),
        ]
        direct[j, c] = [
            y_copy(1, 0, j, c, piece(prv, half, half, j, c), from_next[j].at[c, upper, :, wide]),
            y_copy(1, 1, j, c, piece(nxt, 0, half, j, c), from_prev[j].at[c, lower, :, wide]),
        ]
        onward[j, c] = [
            y_copy(2, 0, j, c, relay[j][0].at[c, :, :, wide], from_next[j].at[c, lower, :, wide]),
            y_copy(2, 1, j, c, relay[j][1].at[c, :, :, wide], from_prev[j].at[c, upper, :, wide]),
        ]

    def start(table, j):
        if j < n:
            for c in range(2):
                for copy in table[j, c]:
                    copy.start()

    pl.semaphore_wait(barrier, shards - 1 + 2)
    start(first, 0)
    start(direct, 0)
    start(first, 1)

    for copy in in_copies[:2]:
        copy.wait()
    tile = 128

    def cast_roots(t, carry):
        at = pl.ds(pl.multiple_of(t * tile, tile), tile)
        lroot[at, :] = lr[at, :].astype(BF16)
        rroot[at, :] = rr[at, :].astype(BF16)
        return carry

    lax.fori_loop(0, block // tile, cast_roots, 0)

    def pass_on(j):
        for c in range(2):
            wide = part(j, c)[1]
            for way in range(2):
                own_copies[j, c][way].wait()
                first[j, c][way].wait_recv()
                buf, mine = relay[j][way], relay_own[j][way]
                both = buf[c, :, :, 0:wide].astype(F32) + mine[c, :, :, 0:wide].astype(F32)
                buf[c, :, :, 0:wide] = both.astype(BF16)
                onward[j, c][way].start()

    def hand_out(j):
        for c in range(2):
            own_copies[j, c][2].wait()
            for way in range(2):
                direct[j, c][way].wait_recv()
                onward[j, c][way].wait_recv()

        def total(d):
            b = inv_ref[d]
            c, i = lax.rem(b, 2), lax.div(b, 2)
            summed = own_p[j][c, i].astype(F32) + from_next[j][c, i].astype(F32) + from_prev[j][c, i].astype(F32)
            return summed.astype(BF16)

        def send(k, carry):
            d = lax.rem(s + k, shards)
            out_p[j][d] = total(d)
            pltpu.make_async_remote_copy(
                src_ref=out_p[j].at[d],
                dst_ref=arrived[j].at[s],
                send_sem=a_send.at[j],
                recv_sem=a_recv.at[j],
                device_id=(r, d),
                device_id_type=MESH,
            ).start()
            return carry

        lax.fori_loop(1, shards, send, 0)
        arrived[j][s] = total(s)

    def others(src, dst, sem):
        return pltpu.make_async_copy(src.at[pl.ds(0, shards - 1)], dst.at[pl.ds(0, shards - 1)], sem)

    for j in range(n):
        pass_on(j)
        start(direct, j + 1)
        start(first, j + 2)
        if j:
            hand_out(j - 1)
    hand_out(n - 1)

    for copy in in_copies[2:]:
        copy.wait()
    own_c = lax.rem(inv_ref[s], 2)
    real = quarter - own_c * block
    chunk_rows = 64
    adam_sq = jnp.zeros((8, width), F32)
    shaped_sq = jnp.zeros((8, block), F32)
    for j in range(n):
        others(out_p[j], arrived[j], a_recv.at[j]).wait()
        cols = slice(j * width, (j + 1) * width)

        def second_step(t, acc):
            at = pl.ds(pl.multiple_of(t * chunk_rows, chunk_rows), chunk_rows)
            g = arrived[j][pl.ds(pl.multiple_of(t * (chunk_rows // 8), 8), chunk_rows // 8)].astype(F32).reshape(chunk_rows, width)
            gb[at, cols] = g.astype(BF16)
            second = BETA_SECOND * sec[at, cols] + (1.0 - BETA_SECOND) * g * g
            sec[at, cols] = second
            adam = g / (jnp.sqrt(second) + EPS_ADAM)
            return acc + jnp.sum((adam * adam).reshape(chunk_rows // 8, 8, width), axis=0)

        adam_sq = lax.fori_loop(0, block // chunk_rows, second_step, adam_sq)

        def shape_step(t, acc):
            at = pl.ds(pl.multiple_of(t * tile, tile), tile)
            left = jnp.dot(lroot[at, :], gb[:, cols], preferred_element_type=F32).astype(BF16)
            both = jnp.dot(left, rroot[cols, :], preferred_element_type=F32)
            if j:
                both = both + shaped[at, :]
            if j == n - 1:
                both = jnp.where(lax.broadcasted_iota(jnp.int32, (tile, block), 1) < real, both, 0.0)
                acc = acc + jnp.sum((both * both).reshape(tile // 8, 8, block), axis=0)
            shaped[at, :] = both
            return acc

        shaped_sq = lax.fori_loop(0, block // tile, shape_step, shaped_sq)

    adam_norm = jnp.sum(jnp.sum(adam_sq, axis=0, keepdims=True), axis=1, keepdims=True)
    shaped_norm = jnp.sum(jnp.sum(shaped_sq, axis=0, keepdims=True), axis=1, keepdims=True)
    scale = jnp.sqrt(adam_norm + EPS_NORM) / jnp.sqrt(shaped_norm + EPS_NORM)

    per = chunk_rows // 8
    turns = shards // per

    def moment_step(k, carry):
        t = lax.rem(lax.div(s, per) + k, turns)
        at = pl.ds(pl.multiple_of(t * chunk_rows, chunk_rows), chunk_rows)
        moment = BETA_MOMENT * mom[at, :] + scale * shaped[at, :]
        mom[at, :] = moment
        back[pl.ds(pl.multiple_of(t * per, per), per)] = (-LEARN_RATE * moment).reshape(per, 8, block).astype(BF16)
        for i in range(per):
            d = t * per + i

            @pl.when(d != s)
            def _():
                pltpu.make_async_remote_copy(
                    src_ref=back.at[d],
                    dst_ref=back_arrived.at[s],
                    send_sem=b_send,
                    recv_sem=b_recv,
                    device_id=(r, d),
                    device_id_type=MESH,
                ).start()

        return carry

    lax.fori_loop(0, turns, moment_step, 0)
    back_arrived[s] = back[s]

    out_copies = [
        pltpu.make_async_copy(src, dst, o_sem.at[i])
        for i, (src, dst) in enumerate(((mom, mom_out), (sec, sec_out), (ls, left_out), (rs, right_out)))
    ]
    out_copies[0].start()
    out_copies[1].start()

    def left_step(t, carry):
        at = pl.ds(pl.multiple_of(t * tile, tile), tile)
        gram = lax.dot_general(gb[at, :], gb[...], (((1,), (1,)), ((), ())), preferred_element_type=F32)
        ls[at, :] = BETA_STAT * ls[at, :] + (1.0 - BETA_STAT) * gram
        return carry

    lax.fori_loop(0, block // tile, left_step, 0)
    out_copies[2].start()

    for t in range(block // tile):
        at = slice(t * tile, (t + 1) * tile)
        gram = lax.dot_general(gb[:, at], gb[...], (((0,), (0,)), ((), ())), preferred_element_type=F32)
        rs[at, :] = BETA_STAT * rs[at, :] + (1.0 - BETA_STAT) * gram
    out_copies[3].start()

    others(back, back_arrived, b_recv).wait()

    def place(i, carry):
        upd[i, :, 0:block] = back_arrived[tab_ref[2 * i]]
        upd[i, :, block:quarter] = back_arrived[tab_ref[2 * i + 1]][:, 0 : quarter - block]
        return carry

    lax.fori_loop(0, rb, place, 0)
    last = pltpu.make_async_copy(upd, upd_out, o_sem.at[4])
    last.start()
    for table in (first, direct, onward):
        for pair in table.values():
            for copy in pair:
                copy.wait_send()
    for j in range(n):
        others(out_p[j], arrived[j], a_send.at[j]).wait()
    others(back, back_arrived, b_send).wait()
    for copy in out_copies:
        copy.wait()
    last.wait()


def per_device(grads, owner_table, momentum, second, left_stat, right_stat, left_root, right_root):
    groups, shards = lax.axis_size("replica"), lax.axis_size("shard")
    _, rb, rows_dev, full_width = grads.shape
    block = left_stat.shape[2]
    quarter = full_width // groups
    n = CHUNKS
    width = block // n
    replica_index = lax.axis_index("replica")
    own_table = lax.dynamic_index_in_dim(owner_table, replica_index, 0, keepdims=False)
    ids = jnp.arange(shards, dtype=jnp.int32)
    inverse = jnp.sum(jnp.where(own_table[None, :] == ids[:, None], ids[None, :], 0), axis=1)
    cfg = (groups, shards, rb, rows_dev, quarter, block, n, width)
    sq = (block, block)
    whole = pltpu.VMEM((2, rb, rows_dev, width), BF16)
    halves = pltpu.VMEM((2, rb // 2, rows_dev, width), BF16)
    slots = pltpu.VMEM((shards, rows_dev, width), BF16)
    wide_slots = pltpu.VMEM((shards, rows_dev, block), BF16)
    dma = pltpu.SemaphoreType.DMA
    any_spec = pl.BlockSpec(memory_space=pl.ANY)
    smem = pl.BlockSpec(memory_space=pltpu.SMEM)
    update, moment_new, second_new, left_new, right_new = pl.pallas_call(
        functools.partial(kernel, cfg),
        name="shampoo_step",
        out_shape=(jax.ShapeDtypeStruct((rb, rows_dev, quarter), BF16),) + (jax.ShapeDtypeStruct(sq, F32),) * 4,
        in_specs=[smem, smem] + [any_spec] * 7,
        out_specs=[any_spec] * 5,
        scratch_shapes=[whole] * (3 * n)
        + [halves] * (4 * n)
        + [slots] * (2 * n)
        + [pltpu.VMEM(sq, F32)] * 6
        + [pltpu.VMEM(sq, BF16)] * 3
        + [pltpu.VMEM(sq, F32), wide_slots, wide_slots, pltpu.VMEM((rb, rows_dev, quarter), BF16)]
        + [dma((6,)), dma((n, 2)), dma((n, 2, 2)), dma((3, 2, n, 2)), dma((3, 2, n, 2)), dma((n,)), dma((n,)), dma, dma, dma((5,))],
        compiler_params=pltpu.CompilerParams(collective_id=1, has_side_effects=True, vmem_limit_bytes=60 * 2**20),
        cost_estimate=pl.CostEstimate(flops=8 * block**3, bytes_accessed=16 * 2**20, transcendentals=0),
    )(inverse, own_table, grads[0], momentum[0, 0], second[0, 0], left_stat[0, 0], right_stat[0, 0], left_root[0, 0], right_root[0, 0])
    shape_own = (1, 1, block, block)
    return (
        update,
        moment_new.reshape(shape_own),
        second_new.reshape(shape_own),
        left_new.reshape(shape_own),
        right_new.reshape(shape_own),
    )


def solution(mesh):
    owned = P("replica", "shard", None, None)
    return jax.shard_map(
        per_device,
        mesh=mesh,
        in_specs=(P("replica", None, "shard", None), P(), owned, owned, owned, owned, owned, owned),
        out_specs=(P(None, "shard", "replica"), owned, owned, owned, owned),
        check_vma=False,
    )
```

time: 223 us -> 69.4 us (0.31)
  local copies, waits for them, and re-layouts: 97.1 us -> 7.87 us
  waiting for transfers between devices: 65.9 us -> 0 us
  Pallas kernels: 0 us -> 60.1 us
  starting transfers between devices: 17.1 us -> 0 us
  between operations: 17.6 us -> 0.67 us
  matrix products: 16.3 us -> 0 us
  other arithmetic: 6.89 us -> 0.63 us
    unnamed x10 -> x15, local copies, waits for them, and re-layouts: 85.6 us -> 7.86 us
    pallas_call x0 -> x1, Pallas kernels: none -> 60.1 us  [per_device(): pl.pallas_call(functools.partial(kernel, cfg), name='shampoo_step', out_s...]
    unnamed x2 -> x0, waiting for transfers between devices: 33.8 us -> none
    all_to_all x2 -> x0, waiting for transfers between devices: 32.2 us -> none  [the longest x1 25.1 us: per_device(): lax.all_to_all(outgoing, 'shard', split_axis=0, concat_axis=0, tiled=True)]
    all_to_all x2 -> x0, starting transfers between devices: 17.1 us -> none  [the longest x1 10.6 us: per_device(): lax.all_to_all(outgoing, 'shard', split_axis=0, concat_axis=0, tiled=True)]
    dot_general x4 -> x0, matrix products: 16.3 us -> none  [the longest x1 4.69 us: per_device(): jnp.dot(left_root[0, 0], grad_block, precision=HIGHEST)]
    gather x2 -> x0, local copies, waits for them, and re-layouts: 8.69 us -> none  [the longest x1 4.86 us: per_device(): outgoing = pieces[row_pick, row_ids[None, :], col_pick, :]]
    reshape x2 -> x0, other arithmetic: 3.05 us -> none  [the longest x1 2.94 us: per_device(): moment_new.reshape(shape_own)]
  transfers between devices with their start and end apart: 3 -> 0, of which waited for: 3 -> 0; matrix products, arithmetic and copies ran while one was open for 5% -> 0% of each run, Pallas kernels for 0% -> 0%
where the time goes in v1:
time: 69.4 us; the launch traced here: 69.2 us
  Pallas kernels  60.1 us (87%)
  local copies, waits for them, and re-layouts  7.87 us (11%)
    pallas_call x1, Pallas kernels, per_device(): pl.pallas_call(functools.partial(kernel, cfg), name='shampoo_step', out_s...  60.1 us
    unnamed x15, local copies, waits for them, and re-layouts  7.86 us

profile of v1, /device:TPU:1, one launch (start us, length us, event | category | flops | bytes accessed | tf_op | source)
XLA Modules:
  0.0 69.2 jit_solution(2657892652143602714)
XLA Ops:
  0.6 0.0 copy-start
  0.7 0.7 copy-done
  1.3 0.0 copy-start.4
  1.3 0.6 select_reduce_fusion.inv_ref
  2.0 0.0 copy-done.4
  2.0 60.1 %shampoo_step.1 = (bf16[32,8,896]{2,1,0:T(8,128)(2,1)}, f32[512,512]{1,0:T(8,128)}, f32[512,512]{1,0:T(8,128)}, f32[512,512]{1,0:T(8,128)}, f32[512,512]{1,0:T(8,128)}) custom-call(s32[64]{0:T(128)} %select_reduce_fusion.inv_ref, s32[64]{0:T(128)} %copy-done.4, bf16[32,8,3584]{2,1,0:T(8,128)(2,1)} %bitcast.13, f32[512,512]{1,0:T(8,128)} %bitcast.14, ...), custom_call_target="tpu_custom_call" | custom-call | flops 1073741824 | bytes 16777216 | tf_op jit(solution)/shard_map/shampoo_step/pallas_call | solution.py:315
  62.0 0.0 copy-start.3
  62.0 1.9 %copy.18 = bf16[32,8,896]{2,1,0:T(8,128)(2,1)} copy(bf16[32,8,896]{2,1,0:T(8,128)(2,1)} %get-tuple-element.20) | data formatting | bytes 917504
  64.0 0.0 copy-start.2
  64.0 2.4 %copy.19 = f32[1,1,512,512]{3,2,1,0:T(8,128)} copy(f32[1,1,512,512]{3,2,1,0:T(8,128)} %bitcast.23) | data formatting | bytes 2097152
  66.3 0.0 copy-done.3
  66.3 0.0 copy-start.1
  66.3 1.0 %copy.20 = f32[1,1,512,512]{3,2,1,0:T(8,128)} copy(f32[1,1,512,512]{3,2,1,0:T(8,128)S(1)} %bitcast.22) | data formatting | bytes 2097152
  67.3 0.0 copy-done.2
  67.3 1.0 %copy.21 = f32[1,1,512,512]{3,2,1,0:T(8,128)} copy(f32[1,1,512,512]{3,2,1,0:T(8,128)S(1)} %bitcast.21) | data formatting | bytes 2097152
  68.3 0.0 copy-done.1
  68.3 1.0 %copy.22 = f32[1,1,512,512]{3,2,1,0:T(8,128)} copy(f32[1,1,512,512]{3,2,1,0:T(8,128)S(1)} %bitcast.20) | data formatting | bytes 2097152
  (1 shorter events, 0.0 us)
Async XLA Ops:
  0.6 0.7 copy-start
  1.3 0.6 copy-start.4
  62.0 4.3 %copy-start.3 = (f32[512,512]{1,0:T(8,128)S(1)}, f32[512,512]{1,0:T(8,128)}, u32[]{:S(2)}) copy-start(f32[512,512]{1,0:T(8,128)} %get-tuple-element.12) | copy-start | bytes 3145732
  64.0 3.3 %copy-start.2 = (f32[512,512]{1,0:T(8,128)S(1)}, f32[512,512]{1,0:T(8,128)}, u32[]{:S(2)}) copy-start(f32[512,512]{1,0:T(8,128)} %get-tuple-element.13) | copy-start | bytes 3145732
  66.3 1.9 %copy-start.1 = (f32[512,512]{1,0:T(8,128)S(1)}, f32[512,512]{1,0:T(8,128)}, u32[]{:S(2)}) copy-start(f32[512,512]{1,0:T(8,128)} %get-tuple-element.14) | copy-start | bytes 3145732

commit v2 on v1

v2 whole, which is shorter than its diff:
```python
import functools

import jax
import jax.numpy as jnp
from jax import lax
from jax.experimental import pallas as pl
from jax.experimental.pallas import tpu as pltpu
from jax.sharding import PartitionSpec as P

BETA_STAT = 0.95
BETA_SECOND = 0.99
BETA_MOMENT = 0.9
EPS_ADAM = 1e-08
EPS_NORM = 1e-06
LEARN_RATE = 0.5
MESH = pl.DeviceIdType.MESH
F32 = jnp.float32
BF16 = jnp.bfloat16
CHUNKS = 4
SPOTS = 8
SPLIT = 4


def kernel(cfg, table_in, g_in, mom_in, sec_in, ls_in, rs_in, lr_in, rr_in, back_arrived, mom, sec, ls, rs, *scratch):
    groups, shards, rb, rows_dev, quarter, block, n, width = cfg
    half = rb // 2
    scratch = list(scratch)

    def take(count):
        got = scratch[:count]
        del scratch[:count]
        return got

    from_next, from_prev, total = take(n), take(n), take(n)
    relay = [take(2) for _ in range(n)]
    out_p, arrived = take(n), take(n)
    lr, rr, lroot, rroot, gb, shaped, back, g_ref, table_ref, inv_v, inv_ref = take(11)
    in_sem, g_sem, inv_sem, y_send, y_recv, a_send, a_recv, b_send, b_recv, near_in, line_in, all_in = take(12)

    r, s = lax.axis_index("replica"), lax.axis_index("shard")
    nxt, prv, opp = lax.rem(r + 1, groups), lax.rem(r + groups - 1, groups), lax.rem(r + 2, groups)

    barrier = pltpu.get_barrier_semaphore()
    plane, spot, planes = lax.div(s, SPOTS), lax.rem(s, SPOTS), shards // SPOTS
    in_plane = [(r, plane * SPOTS + lax.rem(spot + k, SPOTS)) for k in range(1, SPOTS)]
    in_line = [(r, lax.rem(plane + k, planes) * SPOTS + spot) for k in range(planes)]
    near = [(nxt, s), (prv, s), in_line[1], in_line[planes - 1]] + in_plane
    for peer in near:
        pl.semaphore_signal(barrier, inc=1, device_id=peer, device_id_type=MESH)

    def columns(q):
        return pl.ds(pl.multiple_of(q * quarter, 128), quarter)

    g_copies = [
        pltpu.make_async_copy(g_in.at[:, :, columns(q)], g_ref.at[:, :, columns(q)], g_sem.at[i])
        for i, q in enumerate((opp, nxt, prv, r))
    ]
    for copy in g_copies:
        copy.start()

    table_copy = pltpu.make_async_copy(table_in, table_ref, inv_sem.at[0])
    table_copy.start()

    table_copy.wait()
    table = table_ref[pl.ds(r, 1), :]
    rows = lax.broadcasted_iota(jnp.int32, (shards, shards), 0)
    cols = lax.broadcasted_iota(jnp.int32, (shards, shards), 1)
    column = jnp.sum(jnp.where(rows == cols, table, 0), axis=1, keepdims=True)
    inv_v[...] = jnp.zeros_like(inv_v)
    inv_v[:, 0:shards] = jnp.max(jnp.where(column == cols, rows, 0), axis=0, keepdims=True)
    inv_copy = pltpu.make_async_copy(inv_v, inv_ref, inv_sem.at[1])
    inv_copy.start()

    def part(j, c):
        start = c * block + j * width
        return start, max(0, min(width, quarter - start))

    def piece(q, lo, rows, j, c):
        start, wide = part(j, c)
        return g_ref.at[pl.ds(lo, rows), :, pl.ds(pl.multiple_of(q * quarter + start, 128), wide)]

    parts = [(j, c) for j in range(n) for c in range(2) if part(j, c)[1] > 0]
    for j in range(n):
        wide = part(j, 1)[1]
        if wide < width:
            total[j][1, :, :, wide:] = jnp.zeros((rb, rows_dev, width - wide), BF16)
    def y_copy(kind, way, j, c, src, dst):
        return pltpu.make_async_remote_copy(
            src_ref=src,
            dst_ref=dst,
            send_sem=y_send.at[kind, way, j, c],
            recv_sem=y_recv.at[kind, way, j, c],
            device_id=(nxt if way else prv, s),
            device_id_type=MESH,
        )

    first, direct, onward = {}, {}, {}
    for j, c in parts:
        wide = pl.ds(0, part(j, c)[1])
        lower, upper = pl.ds(0, half), pl.ds(half, half)
        first[j, c] = [
            y_copy(0, 0, j, c, piece(opp, 0, half, j, c), relay[j][0].at[c, :, :, wide]),
            y_copy(0, 1, j, c, piece(opp, half, half, j, c), relay[j][1].at[c, :, :, wide]),
        ]
        direct[j, c] = [
            y_copy(1, 0, j, c, piece(prv, half, half, j, c), from_next[j].at[c, upper, :, wide]),
            y_copy(1, 1, j, c, piece(nxt, 0, half, j, c), from_prev[j].at[c, lower, :, wide]),
        ]
        onward[j, c] = [
            y_copy(2, 0, j, c, relay[j][0].at[c, :, :, wide], from_next[j].at[c, lower, :, wide]),
            y_copy(2, 1, j, c, relay[j][1].at[c, :, :, wide], from_prev[j].at[c, upper, :, wide]),
        ]

    def start(table, j):
        if j < n:
            for c in range(2):
                for copy in table.get((j, c), ()):
                    copy.start()

    g_copies[0].wait()
    def tell(peers, sem):
        for peer in peers:
            pl.semaphore_signal(sem, inc=1, device_id=peer, device_id_type=MESH)

    pl.semaphore_wait(barrier, len(near))
    tell((in_line[1], in_line[planes - 1]), near_in)
    for j in range(n):
        start(first, j)
    for copy in g_copies[1:]:
        copy.wait()
    start(direct, 0)
    pl.semaphore_wait(near_in, 2)
    tell((in_line[2], in_line[planes - 2]), line_in)

    in_copies = [
        pltpu.make_async_copy(src, dst, in_sem.at[i])
        for i, (src, dst) in enumerate(((lr_in, lr), (rr_in, rr), (sec_in, sec), (mom_in, mom), (ls_in, ls), (rs_in, rs)))
    ]
    for copy in in_copies:
        copy.start()

    tile = 128

    def mine(q, lo, count, j, c):
        start, wide = part(j, c)
        return g_ref[pl.ds(lo, count), :, pl.ds(pl.multiple_of(q * quarter + start, 128), wide)].astype(F32)

    def pass_on(j):
        for c in range(2):
            wide = part(j, c)[1]
            for way, q, lo in ((0, prv, 0), (1, nxt, half)) if wide else ():
                first[j, c][way].wait_recv()
                buf = relay[j][way]
                buf[c, :, :, 0:wide] = (buf[c, :, :, 0:wide].astype(F32) + mine(q, lo, half, j, c)).astype(BF16)
                onward[j, c][way].start()

    def hand_out(j):
        for c in range(2):
            wide = part(j, c)[1]
            if not wide:
                continue
            for way in range(2):
                direct[j, c][way].wait_recv()
                onward[j, c][way].wait_recv()
            summed = mine(r, 0, rb, j, c) + from_next[j][c, :, :, 0:wide].astype(F32) + from_prev[j][c, :, :, 0:wide].astype(F32)
            total[j][c, :, :, 0:wide] = summed.astype(BF16)

        def block_of(d):
            b = inv_ref[0, d]
            return total[j][lax.rem(b, 2), lax.div(b, 2)]

        def send(k, carry):
            d = lax.rem(s + k, shards)
            out_p[j][d] = block_of(d)
            pltpu.make_async_remote_copy(
                src_ref=out_p[j].at[d],
                dst_ref=arrived[j].at[s],
                send_sem=a_send.at[j],
                recv_sem=a_recv.at[j],
                device_id=(r, d),
                device_id_type=MESH,
            ).start()
            return carry

        lax.fori_loop(1, shards, send, 0, unroll=9)
        arrived[j][s] = block_of(s)

    def others(src, dst, sem):
        return pltpu.make_async_copy(src.at[pl.ds(0, shards - 1)], dst.at[pl.ds(0, shards - 1)], sem)

    inv_copy.wait()
    for j in range(n):
        pass_on(j)
        start(direct, j + 1)
        if j == 0:
            pl.semaphore_wait(line_in, 2)
            tell(in_plane, all_in)
    pl.semaphore_wait(all_in, len(in_plane))
    for j in range(n):
        hand_out(j)

    for copy in in_copies[:2]:
        copy.wait()

    def cast_roots(t, carry):
        at = pl.ds(pl.multiple_of(t * tile, tile), tile)
        lroot[at, :] = lr[at, :].astype(BF16)
        rroot[at, :] = rr[at, :].astype(BF16)
        return carry

    lax.fori_loop(0, block // tile, cast_roots, 0)

    for copy in in_copies[2:]:
        copy.wait()
    own_c = lax.rem(inv_ref[0, s], 2)
    real = quarter - own_c * block
    chunk_rows = 64
    adam_sq = jnp.zeros((8, width), F32)
    shaped_sq = jnp.zeros((8, block), F32)
    for j in range(n):
        others(out_p[j], arrived[j], a_recv.at[j]).wait()
        cols = slice(j * width, (j + 1) * width)

        def second_step(t, acc):
            at = pl.ds(pl.multiple_of(t * chunk_rows, chunk_rows), chunk_rows)
            g = arrived[j][pl.ds(pl.multiple_of(t * (chunk_rows // 8), 8), chunk_rows // 8)].astype(F32).reshape(chunk_rows, width)
            gb[at, cols] = g.astype(BF16)
            second = BETA_SECOND * sec[at, cols] + (1.0 - BETA_SECOND) * g * g
            sec[at, cols] = second
            adam = g / (jnp.sqrt(second) + EPS_ADAM)
            return acc + jnp.sum((adam * adam).reshape(chunk_rows // 8, 8, width), axis=0)

        adam_sq = lax.fori_loop(0, block // chunk_rows, second_step, adam_sq)

        def shape_step(t, acc):
            at = pl.ds(pl.multiple_of(t * tile, tile), tile)
            left = jnp.dot(lroot[at, :], gb[:, cols], preferred_element_type=F32).astype(BF16)
            both = jnp.dot(left, rroot[cols, :], preferred_element_type=F32)
            if j:
                both = both + shaped[at, :]
            if j == n - 1:
                both = jnp.where(lax.broadcasted_iota(jnp.int32, (tile, block), 1) < real, both, 0.0)
                acc = acc + jnp.sum((both * both).reshape(tile // 8, 8, block), axis=0)
            shaped[at, :] = both
            return acc

        shaped_sq = lax.fori_loop(0, block // tile, shape_step, shaped_sq)

    adam_norm = jnp.sum(jnp.sum(adam_sq, axis=0, keepdims=True), axis=1, keepdims=True)
    shaped_norm = jnp.sum(jnp.sum(shaped_sq, axis=0, keepdims=True), axis=1, keepdims=True)
    scale = jnp.sqrt(adam_norm + EPS_NORM) / jnp.sqrt(shaped_norm + EPS_NORM)

    per = chunk_rows // 8
    turns = shards // per

    def moment_step(k, carry):
        t = lax.rem(lax.div(s, per) + k, turns)
        at = pl.ds(pl.multiple_of(t * chunk_rows, chunk_rows), chunk_rows)
        moment = BETA_MOMENT * mom[at, :] + scale * shaped[at, :]
        mom[at, :] = moment
        back[pl.ds(pl.multiple_of(t * per, per), per)] = (-LEARN_RATE * moment).reshape(per, 8, block).astype(BF16)
        for i in range(per):
            d = t * per + i

            @pl.when(d != s)
            def _():
                pltpu.make_async_remote_copy(
                    src_ref=back.at[d],
                    dst_ref=back_arrived.at[s],
                    send_sem=b_send,
                    recv_sem=b_recv,
                    device_id=(r, d),
                    device_id_type=MESH,
                ).start()

        return carry

    lax.fori_loop(0, turns, moment_step, 0)
    back_arrived[s] = back[s]

    def left_step(t, carry):
        at = pl.ds(pl.multiple_of(t * tile, tile), tile)
        gram = lax.dot_general(gb[at, :], gb[...], (((1,), (1,)), ((), ())), preferred_element_type=F32)
        ls[at, :] = BETA_STAT * ls[at, :] + (1.0 - BETA_STAT) * gram
        return carry

    lax.fori_loop(0, block // tile, left_step, 0)

    for t in range(block // tile):
        at = slice(t * tile, (t + 1) * tile)
        gram = lax.dot_general(gb[:, at], gb[...], (((0,), (0,)), ((), ())), preferred_element_type=F32)
        rs[at, :] = BETA_STAT * rs[at, :] + (1.0 - BETA_STAT) * gram

    others(back, back_arrived, b_recv).wait()

    for table in (first, direct, onward):
        for pair in table.values():
            for copy in pair:
                copy.wait_send()
    for j in range(n):
        others(out_p[j], arrived[j], a_send.at[j]).wait()
    others(back, back_arrived, b_send).wait()


def finish(quarter, block, table_ref, arrived, mom, sec, ls, rs, upd_out, mom_out, sec_out, left_out, right_out, upd, sem):
    pairs = ((mom, mom_out), (sec, sec_out), (ls, left_out), (rs, right_out))
    rows = block // SPLIT
    copies = [
        pltpu.make_async_copy(src.at[pl.ds(k * rows, rows)], dst.at[pl.ds(k * rows, rows)], sem.at[i * SPLIT + k])
        for i, (src, dst) in enumerate(pairs)
        for k in range(SPLIT)
    ]
    for copy in copies:
        copy.start()

    r = lax.axis_index("replica")

    def place(i, carry):
        upd[i, :, 0:block] = arrived[table_ref[r, 2 * i]]
        upd[i, :, block:quarter] = arrived[table_ref[r, 2 * i + 1]][:, 0 : quarter - block]
        return carry

    lax.fori_loop(0, upd.shape[0], place, 0)
    last = pltpu.make_async_copy(upd, upd_out, sem.at[4 * SPLIT])
    last.start()
    for copy in copies:
        copy.wait()
    last.wait()


def per_device(grads, owner_table, momentum, second, left_stat, right_stat, left_root, right_root):
    groups, shards = lax.axis_size("replica"), lax.axis_size("shard")
    _, rb, rows_dev, full_width = grads.shape
    block = left_stat.shape[2]
    quarter = full_width // groups
    n = CHUNKS
    width = block // n
    cfg = (groups, shards, rb, rows_dev, quarter, block, n, width)
    sq = (block, block)
    whole = pltpu.VMEM((2, rb, rows_dev, width), BF16)
    halves = pltpu.VMEM((2, rb // 2, rows_dev, width), BF16)
    slots = pltpu.VMEM((shards, rows_dev, width), BF16)
    wide_slots = pltpu.VMEM((shards, rows_dev, block), BF16)
    dma = pltpu.SemaphoreType.DMA
    hbm = pl.BlockSpec(memory_space=pltpu.HBM)
    vmem = pl.BlockSpec(memory_space=pltpu.VMEM)
    smem = pl.BlockSpec(memory_space=pltpu.SMEM)
    operands = (owner_table, grads[0], *[a[0, 0] for a in (momentum, second, left_stat, right_stat, left_root, right_root)])
    results = pl.pallas_call(
        functools.partial(kernel, cfg),
        name="shampoo_step",
        out_shape=(pltpu.VMEM((shards, rows_dev, block), BF16),) + (pltpu.VMEM(sq, F32),) * 4,
        in_specs=[hbm] * 8,
        out_specs=[vmem] * 5,
        scratch_shapes=[whole] * (3 * n)
        + [halves] * (2 * n)
        + [slots] * (2 * n)
        + [pltpu.VMEM(sq, F32)] * 2
        + [pltpu.VMEM(sq, BF16)] * 3
        + [pltpu.VMEM(sq, F32), wide_slots, pltpu.VMEM((rb, rows_dev, full_width), BF16)]
        + [pltpu.VMEM(owner_table.shape, jnp.int32), pltpu.VMEM((1, 128), jnp.int32), pltpu.SMEM((1, 128), jnp.int32)]
        + [dma((6,)), dma((4,)), dma((2,)), dma((3, 2, n, 2)), dma((3, 2, n, 2)), dma((n,)), dma((n,)), dma, dma] + [pltpu.SemaphoreType.REGULAR] * 3,
        compiler_params=pltpu.CompilerParams(collective_id=1, has_side_effects=True, vmem_limit_bytes=40 * 2**20),
        cost_estimate=pl.CostEstimate(flops=8 * block**3, bytes_accessed=16 * 2**20, transcendentals=0),
    )(*[pltpu.with_memory_space_constraint(a, pltpu.HBM) for a in operands])
    update, moment_new, second_new, left_new, right_new = pl.pallas_call(
        functools.partial(finish, quarter, block),
        name="place_update",
        out_shape=(jax.ShapeDtypeStruct((rb, rows_dev, quarter), BF16),) + (jax.ShapeDtypeStruct(sq, F32),) * 4,
        in_specs=[smem] + [vmem] * 5,
        out_specs=[hbm] * 5,
        scratch_shapes=[pltpu.VMEM((rb, rows_dev, quarter), BF16), dma((4 * SPLIT + 1,))],
        compiler_params=pltpu.CompilerParams(vmem_limit_bytes=8 * 2**20),
    )(owner_table, *results)
    shape_own = (1, 1, block, block)
    return (
        update,
        moment_new.reshape(shape_own),
        second_new.reshape(shape_own),
        left_new.reshape(shape_own),
        right_new.reshape(shape_own),
    )


def solution(mesh):
    owned = P("replica", "shard", None, None)
    return jax.shard_map(
        per_device,
        mesh=mesh,
        in_specs=(P("replica", None, "shard", None), P(), owned, owned, owned, owned, owned, owned),
        out_specs=(P(None, "shard", "replica"), owned, owned, owned, owned),
        check_vma=False,
    )
```

time: 69.4 us -> 57 us (0.82)
  the two profiles are of different devices: /device:TPU:1 before, /device:TPU:7 now
where the time goes in v2:
time: 57 us; the launch traced here: 56.9 us
  Pallas kernels  56.2 us (99%)
  between operations  0.66 us (1%)
    pallas_call x1, Pallas kernels, per_device(): pl.pallas_call(functools.partial(kernel, cfg), name='shampoo_step', out_s...  53.3 us
    pallas_call x1, Pallas kernels, per_device(): pl.pallas_call(functools.partial(finish, quarter, block), name='place_upd...  2.86 us

profile of v2, /device:TPU:7, one launch (start us, length us, event | category | flops | bytes accessed | tf_op | source)
XLA Modules:
  0.0 56.9 jit_solution(10761429057652094407)
XLA Ops:
  0.6 0.0 copy-start
  0.6 53.3 %shampoo_step.1 = (bf16[64,8,512]{2,1,0:T(8,128)(2,1)S(1)}, f32[512,512]{1,0:T(8,128)S(1)}, f32[512,512]{1,0:T(8,128)S(1)}, f32[512,512]{1,0:T(8,128)S(1)}, f32[512,512]{1,0:T(8,128)S(1)}) custom-call(s32[4,64]{1,0:T(4,128)} %table_ref.1, bf16[32,8,3584]{2,1,0:T(8,128)(2,1)} %bitcast.11, f32[512,512]{1,0:T(8,128)} %bitcast.12, f32[512,512]{1,0:T(8,128)} %bitcast.13, ...), custom_call_target="tpu_custom_call" | custom-call | flops 1073741824 | bytes 16777216 | tf_op jit(solution)/shard_map/shampoo_step/pallas_call | solution.py:349
  54.0 0.0 copy-done
  54.0 2.9 %place_update.1 = (bf16[32,8,896]{2,1,0:T(8,128)(2,1)}, f32[512,512]{1,0:T(8,128)}, f32[512,512]{1,0:T(8,128)}, f32[512,512]{1,0:T(8,128)}, f32[512,512]{1,0:T(8,128)}) custom-call(s32[4,64]{1,0:T(4,128)S(1)} %copy-done, bf16[64,8,512]{2,1,0:T(8,128)(2,1)S(1)} %get-tuple-element.15.arrived, f32[512,512]{1,0:T(8,128)S(1)} %get-tuple-element.16.mom, ...), custom_call_target="tpu_custom_call" | custom-call | tf_op jit(solution)/shard_map/place_update/pallas_call | solution.py:366
Async XLA Ops:
  0.6 53.4 %copy-start = (s32[4,64]{1,0:T(4,128)S(1)}, s32[4,64]{1,0:T(4,128)}, u32[]{:S(2)}) copy-start(s32[4,64]{1,0:T(4,128)} %table_ref.1) | copy-start | bytes 3076

commit v3 on v2

--- a/solution.py
+++ b/solution.py
@@ -18,7 +18,7 @@
 BF16 = jnp.bfloat16
 CHUNKS = 4
 SPOTS = 8
-SPLIT = 4
+SPLIT = 1
 
 
 def kernel(cfg, table_in, g_in, mom_in, sec_in, ls_in, rs_in, lr_in, rr_in, back_arrived, mom, sec, ls, rs, *scratch):
@@ -33,9 +33,10 @@
 
     from_next, from_prev, total = take(n), take(n), take(n)
     relay = [take(2) for _ in range(n)]
+    (from_opp,) = take(1)
     out_p, arrived = take(n), take(n)
     lr, rr, lroot, rroot, gb, shaped, back, g_ref, table_ref, inv_v, inv_ref = take(11)
-    in_sem, g_sem, inv_sem, y_send, y_recv, a_send, a_recv, b_send, b_recv, near_in, line_in, all_in = take(12)
+    in_sem, g_sem, inv_sem, d_send, d_recv, y_send, y_recv, a_send, a_recv, b_send, b_recv, near_in, line_in, all_in = take(14)
 
     r, s = lax.axis_index("replica"), lax.axis_index("shard")
     nxt, prv, opp = lax.rem(r + 1, groups), lax.rem(r + groups - 1, groups), lax.rem(r + 2, groups)
@@ -44,33 +45,30 @@
     plane, spot, planes = lax.div(s, SPOTS), lax.rem(s, SPOTS), shards // SPOTS
     in_plane = [(r, plane * SPOTS + lax.rem(spot + k, SPOTS)) for k in range(1, SPOTS)]
     in_line = [(r, lax.rem(plane + k, planes) * SPOTS + spot) for k in range(planes)]
-    near = [(nxt, s), (prv, s), in_line[1], in_line[planes - 1]] + in_plane
-    for peer in near:
-        pl.semaphore_signal(barrier, inc=1, device_id=peer, device_id_type=MESH)
-
-    def columns(q):
-        return pl.ds(pl.multiple_of(q * quarter, 128), quarter)
-
-    g_copies = [
-        pltpu.make_async_copy(g_in.at[:, :, columns(q)], g_ref.at[:, :, columns(q)], g_sem.at[i])
-        for i, q in enumerate((opp, nxt, prv, r))
-    ]
-    for copy in g_copies:
-        copy.start()
-
+    near = [(nxt, s), (prv, s), (opp, s), in_line[1], in_line[planes - 1]] + in_plane
+    def greet(peers):
+        for peer in peers:
+            pl.semaphore_signal(barrier, inc=1, device_id=peer, device_id_type=MESH)
+
+    greet(near[:3])
+
+    early, late = n - 1, list(range(n - 1))
+    spans = [(early * width, width), (0, early * width), (block, quarter - block)]
+
+    def load(i, q, k):
+        lo, wide = spans[k]
+        at = pl.ds(pl.multiple_of(q * quarter + lo, 128), wide)
+        return pltpu.make_async_copy(g_in.at[:, :, at], g_ref.at[:, :, at], g_sem.at[i, k])
+
+    loads = [[load(i, q, k) for k in range(3)] for i, q in enumerate((opp, nxt, prv, r))]
+    for i in range(3):
+        loads[i][0].start()
+    greet(near[3:])
+    for i in range(4):
+        for k in range(1 if i < 3 else 0, 3):
+            loads[i][k].start()
     table_copy = pltpu.make_async_copy(table_in, table_ref, inv_sem.at[0])
     table_copy.start()
-
-    table_copy.wait()
-    table = table_ref[pl.ds(r, 1), :]
-    rows = lax.broadcasted_iota(jnp.int32, (shards, shards), 0)
-    cols = lax.broadcasted_iota(jnp.int32, (shards, shards), 1)
-    column = jnp.sum(jnp.where(rows == cols, table, 0), axis=1, keepdims=True)
-    inv_v[...] = jnp.zeros_like(inv_v)
-    inv_v[:, 0:shards] = jnp.max(jnp.where(column == cols, rows, 0), axis=0, keepdims=True)
-    inv_copy = pltpu.make_async_copy(inv_v, inv_ref, inv_sem.at[1])
-    inv_copy.start()
-
     def part(j, c):
         start = c * block + j * width
         return start, max(0, min(width, quarter - start))
@@ -96,6 +94,8 @@
 
     first, direct, onward = {}, {}, {}
     for j, c in parts:
+        if j == n - 1:
+            continue
         wide = pl.ds(0, part(j, c)[1])
         lower, upper = pl.ds(0, half), pl.ds(half, half)
         first[j, c] = [
@@ -111,26 +111,59 @@
             y_copy(2, 1, j, c, relay[j][1].at[c, :, :, wide], from_prev[j].at[c, upper, :, wide]),
         ]
 
+    straight = [
+        pltpu.make_async_remote_copy(
+            src_ref=piece(q, 0, rb, early, c),
+            dst_ref=buf.at[c, :, :, pl.ds(0, part(early, c)[1])],
+            send_sem=d_send.at[i, c],
+            recv_sem=d_recv.at[i, c],
+            device_id=(q, s),
+            device_id_type=MESH,
+        )
+        for i, (q, buf) in enumerate(((opp, from_opp), (nxt, from_prev[early]), (prv, from_next[early])))
+        for c in range(2)
+        if part(early, c)[1]
+    ]
+
     def start(table, j):
         if j < n:
             for c in range(2):
                 for copy in table.get((j, c), ()):
                     copy.start()
 
-    g_copies[0].wait()
     def tell(peers, sem):
         for peer in peers:
             pl.semaphore_signal(sem, inc=1, device_id=peer, device_id_type=MESH)
 
+    for i in range(3):
+        loads[i][0].wait()
     pl.semaphore_wait(barrier, len(near))
     tell((in_line[1], in_line[planes - 1]), near_in)
-    for j in range(n):
+    for copy in straight:
+        copy.start()
+    for copy in loads[0][1:]:
+        copy.wait()
+    for j in late:
         start(first, j)
-    for copy in g_copies[1:]:
+    for copy in loads[1][1:] + loads[2][1:]:
         copy.wait()
     start(direct, 0)
+    for copy in loads[3]:
+        copy.wait()
+    table_copy.wait()
+    table = table_ref[pl.ds(r, 1), :]
+    rows = lax.broadcasted_iota(jnp.int32, (shards, shards), 0)
+    cols = lax.broadcasted_iota(jnp.int32, (shards, shards), 1)
+    column = jnp.sum(jnp.where(rows == cols, table, 0), axis=1, keepdims=True)
+    inv_v[...] = jnp.zeros_like(inv_v)
+    inv_v[:, 0:shards] = jnp.max(jnp.where(column == cols, rows, 0), axis=0, keepdims=True)
+    inv_copy = pltpu.make_async_copy(inv_v, inv_ref, inv_sem.at[1])
+    inv_copy.start()
+
     pl.semaphore_wait(near_in, 2)
     tell((in_line[2], in_line[planes - 2]), line_in)
+    pl.semaphore_wait(line_in, 2)
+    tell(in_plane, all_in)
 
     in_copies = [
         pltpu.make_async_copy(src, dst, in_sem.at[i])
@@ -155,14 +188,20 @@
                 onward[j, c][way].start()
 
     def hand_out(j):
+        if j == early:
+            for copy in straight:
+                copy.wait_recv()
         for c in range(2):
             wide = part(j, c)[1]
             if not wide:
                 continue
-            for way in range(2):
-                direct[j, c][way].wait_recv()
-                onward[j, c][way].wait_recv()
+            if j != early:
+                for way in range(2):
+                    direct[j, c][way].wait_recv()
+                    onward[j, c][way].wait_recv()
             summed = mine(r, 0, rb, j, c) + from_next[j][c, :, :, 0:wide].astype(F32) + from_prev[j][c, :, :, 0:wide].astype(F32)
+            if j == early:
+                summed = summed + from_opp[c, :, :, 0:wide].astype(F32)
             total[j][c, :, :, 0:wide] = summed.astype(BF16)
 
         def block_of(d):
@@ -189,14 +228,13 @@
         return pltpu.make_async_copy(src.at[pl.ds(0, shards - 1)], dst.at[pl.ds(0, shards - 1)], sem)
 
     inv_copy.wait()
-    for j in range(n):
+    for j in late:
         pass_on(j)
         start(direct, j + 1)
-        if j == 0:
-            pl.semaphore_wait(line_in, 2)
-            tell(in_plane, all_in)
-    pl.semaphore_wait(all_in, len(in_plane))
-    for j in range(n):
+        if j == min(1, late[-1]):
+            pl.semaphore_wait(all_in, len(in_plane))
+            hand_out(early)
+    for j in late:
         hand_out(j)
 
     for copy in in_copies[:2]:
@@ -217,7 +255,7 @@
     chunk_rows = 64
     adam_sq = jnp.zeros((8, width), F32)
     shaped_sq = jnp.zeros((8, block), F32)
-    for j in range(n):
+    for j in [early] + late:
         others(out_p[j], arrived[j], a_recv.at[j]).wait()
         cols = slice(j * width, (j + 1) * width)
 
@@ -230,21 +268,21 @@
             adam = g / (jnp.sqrt(second) + EPS_ADAM)
             return acc + jnp.sum((adam * adam).reshape(chunk_rows // 8, 8, width), axis=0)
 
-        adam_sq = lax.fori_loop(0, block // chunk_rows, second_step, adam_sq)
+        adam_sq = lax.fori_loop(0, block // chunk_rows, second_step, adam_sq, unroll=True)
 
         def shape_step(t, acc):
             at = pl.ds(pl.multiple_of(t * tile, tile), tile)
             left = jnp.dot(lroot[at, :], gb[:, cols], preferred_element_type=F32).astype(BF16)
             both = jnp.dot(left, rroot[cols, :], preferred_element_type=F32)
-            if j:
+            if j != early:
                 both = both + shaped[at, :]
-            if j == n - 1:
+            if j == late[-1]:
                 both = jnp.where(lax.broadcasted_iota(jnp.int32, (tile, block), 1) < real, both, 0.0)
                 acc = acc + jnp.sum((both * both).reshape(tile // 8, 8, block), axis=0)
             shaped[at, :] = both
             return acc
 
-        shaped_sq = lax.fori_loop(0, block // tile, shape_step, shaped_sq)
+        shaped_sq = lax.fori_loop(0, block // tile, shape_step, shaped_sq, unroll=True)
 
     adam_norm = jnp.sum(jnp.sum(adam_sq, axis=0, keepdims=True), axis=1, keepdims=True)
     shaped_norm = jnp.sum(jnp.sum(shaped_sq, axis=0, keepdims=True), axis=1, keepdims=True)
@@ -293,6 +331,8 @@
 
     others(back, back_arrived, b_recv).wait()
 
+    for copy in straight:
+        copy.wait_send()
     for table in (first, direct, onward):
         for pair in table.values():
             for copy in pair:
@@ -302,7 +342,9 @@
     others(back, back_arrived, b_send).wait()
 
 
-def finish(quarter, block, table_ref, arrived, mom, sec, ls, rs, upd_out, mom_out, sec_out, left_out, right_out, upd, sem):
+def finish(quarter, block, table_in, arrived, mom, sec, ls, rs, upd_out, mom_out, sec_out, left_out, right_out, upd, table_ref, sem, table_sem):
+    table_copy = pltpu.make_async_copy(table_in, table_ref, table_sem)
+    table_copy.start()
     pairs = ((mom, mom_out), (sec, sec_out), (ls, left_out), (rs, right_out))
     rows = block // SPLIT
     copies = [
@@ -314,6 +356,7 @@
         copy.start()
 
     r = lax.axis_index("replica")
+    table_copy.wait()
 
     def place(i, carry):
         upd[i, :, 0:block] = arrived[table_ref[r, 2 * i]]
@@ -344,7 +387,6 @@
     dma = pltpu.SemaphoreType.DMA
     hbm = pl.BlockSpec(memory_space=pltpu.HBM)
     vmem = pl.BlockSpec(memory_space=pltpu.VMEM)
-    smem = pl.BlockSpec(memory_space=pltpu.SMEM)
     operands = (owner_table, grads[0], *[a[0, 0] for a in (momentum, second, left_stat, right_stat, left_root, right_root)])
     results = pl.pallas_call(
         functools.partial(kernel, cfg),
@@ -354,12 +396,13 @@
         out_specs=[vmem] * 5,
         scratch_shapes=[whole] * (3 * n)
         + [halves] * (2 * n)
+        + [whole]
         + [slots] * (2 * n)
         + [pltpu.VMEM(sq, F32)] * 2
         + [pltpu.VMEM(sq, BF16)] * 3
         + [pltpu.VMEM(sq, F32), wide_slots, pltpu.VMEM((rb, rows_dev, full_width), BF16)]
         + [pltpu.VMEM(owner_table.shape, jnp.int32), pltpu.VMEM((1, 128), jnp.int32), pltpu.SMEM((1, 128), jnp.int32)]
-        + [dma((6,)), dma((4,)), dma((2,)), dma((3, 2, n, 2)), dma((3, 2, n, 2)), dma((n,)), dma((n,)), dma, dma] + [pltpu.SemaphoreType.REGULAR] * 3,
+        + [dma((6,)), dma((4, 3)), dma((2,)), dma((3, 2)), dma((3, 2)), dma((3, 2, n, 2)), dma((3, 2, n, 2)), dma((n,)), dma((n,)), dma, dma] + [pltpu.SemaphoreType.REGULAR] * 3,
         compiler_params=pltpu.CompilerParams(collective_id=1, has_side_effects=True, vmem_limit_bytes=40 * 2**20),
         cost_estimate=pl.CostEstimate(flops=8 * block**3, bytes_accessed=16 * 2**20, transcendentals=0),
     )(*[pltpu.with_memory_space_constraint(a, pltpu.HBM) for a in operands])
@@ -367,11 +410,11 @@
         functools.partial(finish, quarter, block),
         name="place_update",
         out_shape=(jax.ShapeDtypeStruct((rb, rows_dev, quarter), BF16),) + (jax.ShapeDtypeStruct(sq, F32),) * 4,
-        in_specs=[smem] + [vmem] * 5,
+        in_specs=[hbm] + [vmem] * 5,
         out_specs=[hbm] * 5,
-        scratch_shapes=[pltpu.VMEM((rb, rows_dev, quarter), BF16), dma((4 * SPLIT + 1,))],
+        scratch_shapes=[pltpu.VMEM((rb, rows_dev, quarter), BF16), pltpu.SMEM(owner_table.shape, jnp.int32), dma((4 * SPLIT + 1,)), dma],
         compiler_params=pltpu.CompilerParams(vmem_limit_bytes=8 * 2**20),
-    )(owner_table, *results)
+    )(pltpu.with_memory_space_constraint(owner_table, pltpu.HBM), *results)
     shape_own = (1, 1, block, block)
     return (
         update,

time: 57 us -> 54.3 us (0.953)
  the two profiles are of different devices: /device:TPU:7 before, /device:TPU:1 now
where the time goes in v3:
time: 54.3 us; the launch traced here: 54.1 us
  Pallas kernels  53.5 us (99%)
  between operations  0.64 us (1%)
    pallas_call x1, Pallas kernels, per_device(): pl.pallas_call(functools.partial(kernel, cfg), name='shampoo_step', out_s...  51.3 us
    pallas_call x1, Pallas kernels, per_device(): pl.pallas_call(functools.partial(finish, quarter, block), name='place_upd...  2.2 us

profile of v3, /device:TPU:1, one launch (start us, length us, event | category | flops | bytes accessed | tf_op | source)
XLA Modules:
  0.0 54.1 jit_solution(9659577032412260553)
XLA Ops:
  0.6 51.3 %shampoo_step.1 = (bf16[64,8,512]{2,1,0:T(8,128)(2,1)S(1)}, f32[512,512]{1,0:T(8,128)S(1)}, f32[512,512]{1,0:T(8,128)S(1)}, f32[512,512]{1,0:T(8,128)S(1)}, f32[512,512]{1,0:T(8,128)S(1)}) custom-call(s32[4,64]{1,0:T(4,128)} %table_in.3, bf16[32,8,3584]{2,1,0:T(8,128)(2,1)} %bitcast.11, f32[512,512]{1,0:T(8,128)} %bitcast.12, f32[512,512]{1,0:T(8,128)} %bitcast.13, ...), custom_call_target="tpu_custom_call" | custom-call | flops 1073741824 | bytes 16777216 | tf_op jit(solution)/shard_map/shampoo_step/pallas_call | solution.py:391
  51.9 2.2 %place_update.1 = (bf16[32,8,896]{2,1,0:T(8,128)(2,1)}, f32[512,512]{1,0:T(8,128)}, f32[512,512]{1,0:T(8,128)}, f32[512,512]{1,0:T(8,128)}, f32[512,512]{1,0:T(8,128)}) custom-call(s32[4,64]{1,0:T(4,128)} %table_in.3, bf16[64,8,512]{2,1,0:T(8,128)(2,1)S(1)} %get-tuple-element.15.arrived, f32[512,512]{1,0:T(8,128)S(1)} %get-tuple-element.16.mom, ...), custom_call_target="tpu_custom_call" | custom-call | tf_op jit(solution)/shard_map/place_update/pallas_call | solution.py:409

commit v4 on v3

--- a/solution.py
+++ b/solution.py
@@ -187,6 +187,12 @@
                 buf[c, :, :, 0:wide] = (buf[c, :, :, 0:wide].astype(F32) + mine(q, lo, half, j, c)).astype(BF16)
                 onward[j, c][way].start()
 
+    def target(k):
+        turn, spot_k = lax.div(k, SPOTS), lax.rem(k, SPOTS)
+        far = lax.div(turn + 1, 2)
+        off = planes // 2 + far * (1 - 2 * lax.rem(turn, 2))
+        return lax.rem(plane + off, planes) * SPOTS + lax.rem(spot + 1 + spot_k, SPOTS)
+
     def hand_out(j):
         if j == early:
             for copy in straight:
@@ -209,7 +215,7 @@
             return total[j][lax.rem(b, 2), lax.div(b, 2)]
 
         def send(k, carry):
-            d = lax.rem(s + k, shards)
+            d = target(k)
             out_p[j][d] = block_of(d)
             pltpu.make_async_remote_copy(
                 src_ref=out_p[j].at[d],
@@ -221,7 +227,7 @@
             ).start()
             return carry
 
-        lax.fori_loop(1, shards, send, 0, unroll=9)
+        lax.fori_loop(0, shards - 1, send, 0, unroll=9)
         arrived[j][s] = block_of(s)
 
     def others(src, dst, sem):
@@ -292,7 +298,8 @@
     turns = shards // per
 
     def moment_step(k, carry):
-        t = lax.rem(lax.div(s, per) + k, turns)
+        far = lax.div(k + 1, 2)
+        t = lax.rem(lax.div(s, per) + turns // 2 + far * (1 - 2 * lax.rem(k, 2)), turns)
         at = pl.ds(pl.multiple_of(t * chunk_rows, chunk_rows), chunk_rows)
         moment = BETA_MOMENT * mom[at, :] + scale * shaped[at, :]
         mom[at, :] = moment
@@ -313,7 +320,7 @@
 
         return carry
 
-    lax.fori_loop(0, turns, moment_step, 0)
+    lax.fori_loop(0, turns, moment_step, 0, unroll=True)
     back_arrived[s] = back[s]
 
     def left_step(t, carry):

time: 54.3 us -> 53.5 us (0.985)
  Pallas kernels: 53.5 us -> 52.7 us
    pallas_call x1, Pallas kernels: 51.3 us -> 50.5 us  [per_device(): pl.pallas_call(functools.partial(kernel, cfg), name='shampoo_step', out_s...]
where the time goes in v4:
time: 53.5 us; the launch traced here: 53.4 us
  Pallas kernels  52.7 us (99%)
  between operations  0.64 us (1%)
    pallas_call x1, Pallas kernels, per_device(): pl.pallas_call(functools.partial(kernel, cfg), name='shampoo_step', out_s...  50.5 us
    pallas_call x1, Pallas kernels, per_device(): pl.pallas_call(functools.partial(finish, quarter, block), name='place_upd...  2.2 us

profile of v4, /device:TPU:1, one launch (start us, length us, event | category | flops | bytes accessed | tf_op | source)
XLA Modules:
  0.0 53.4 jit_solution(5099638243912887368)
XLA Ops:
  0.6 50.5 %shampoo_step.1 = (bf16[64,8,512]{2,1,0:T(8,128)(2,1)S(1)}, f32[512,512]{1,0:T(8,128)S(1)}, f32[512,512]{1,0:T(8,128)S(1)}, f32[512,512]{1,0:T(8,128)S(1)}, f32[512,512]{1,0:T(8,128)S(1)}) custom-call(s32[4,64]{1,0:T(4,128)} %table_in.3, bf16[32,8,3584]{2,1,0:T(8,128)(2,1)} %bitcast.11, f32[512,512]{1,0:T(8,128)} %bitcast.12, f32[512,512]{1,0:T(8,128)} %bitcast.13, ...), custom_call_target="tpu_custom_call" | custom-call | flops 1073741824 | bytes 16777216 | tf_op jit(solution)/shard_map/shampoo_step/pallas_call | solution.py:398
  51.2 2.2 %place_update.1 = (bf16[32,8,896]{2,1,0:T(8,128)(2,1)}, f32[512,512]{1,0:T(8,128)}, f32[512,512]{1,0:T(8,128)}, f32[512,512]{1,0:T(8,128)}, f32[512,512]{1,0:T(8,128)}) custom-call(s32[4,64]{1,0:T(4,128)} %table_in.3, bf16[64,8,512]{2,1,0:T(8,128)(2,1)S(1)} %get-tuple-element.15.arrived, f32[512,512]{1,0:T(8,128)S(1)} %get-tuple-element.16.mom, ...), custom_call_target="tpu_custom_call" | custom-call | tf_op jit(solution)/shard_map/place_update/pallas_call | solution.py:416

commit v5 on v4

--- a/solution.py
+++ b/solution.py
@@ -336,8 +336,6 @@
         gram = lax.dot_general(gb[:, at], gb[...], (((0,), (0,)), ((), ())), preferred_element_type=F32)
         rs[at, :] = BETA_STAT * rs[at, :] + (1.0 - BETA_STAT) * gram
 
-    others(back, back_arrived, b_recv).wait()
-
     for copy in straight:
         copy.wait_send()
     for table in (first, direct, onward):
@@ -347,6 +345,7 @@
     for j in range(n):
         others(out_p[j], arrived[j], a_send.at[j]).wait()
     others(back, back_arrived, b_send).wait()
+    others(back, back_arrived, b_recv).wait()
 
 
 def finish(quarter, block, table_in, arrived, mom, sec, ls, rs, upd_out, mom_out, sec_out, left_out, right_out, upd, table_ref, sem, table_sem):

time: 53.5 us -> 53.5 us (level)
  no operation moved by 1% of the time
where the time goes in v5:
time: 53.5 us; the launch traced here: 53.3 us
  Pallas kernels  52.7 us (99%)
  between operations  0.64 us (1%)
    pallas_call x1, Pallas kernels, per_device(): pl.pallas_call(functools.partial(kernel, cfg), name='shampoo_step', out_s...  50.5 us
    pallas_call x1, Pallas kernels, per_device(): pl.pallas_call(functools.partial(finish, quarter, block), name='place_upd...  2.2 us

profile of v5, /device:TPU:1, one launch (start us, length us, event | category | flops | bytes accessed | tf_op | source)
XLA Modules:
  0.0 53.3 jit_solution(4766216331016013252)
XLA Ops:
  0.6 50.5 %shampoo_step.1 = (bf16[64,8,512]{2,1,0:T(8,128)(2,1)S(1)}, f32[512,512]{1,0:T(8,128)S(1)}, f32[512,512]{1,0:T(8,128)S(1)}, f32[512,512]{1,0:T(8,128)S(1)}, f32[512,512]{1,0:T(8,128)S(1)}) custom-call(s32[4,64]{1,0:T(4,128)} %table_in.3, bf16[32,8,3584]{2,1,0:T(8,128)(2,1)} %bitcast.11, f32[512,512]{1,0:T(8,128)} %bitcast.12, f32[512,512]{1,0:T(8,128)} %bitcast.13, ...), custom_call_target="tpu_custom_call" | custom-call | flops 1073741824 | bytes 16777216 | tf_op jit(solution)/shard_map/shampoo_step/pallas_call | solution.py:397
  51.1 2.2 %place_update.1 = (bf16[32,8,896]{2,1,0:T(8,128)(2,1)}, f32[512,512]{1,0:T(8,128)}, f32[512,512]{1,0:T(8,128)}, f32[512,512]{1,0:T(8,128)}, f32[512,512]{1,0:T(8,128)}) custom-call(s32[4,64]{1,0:T(4,128)} %table_in.3, bf16[64,8,512]{2,1,0:T(8,128)(2,1)S(1)} %get-tuple-element.15.arrived, f32[512,512]{1,0:T(8,128)S(1)} %get-tuple-element.16.mom, ...), custom_call_target="tpu_custom_call" | custom-call | tf_op jit(solution)/shard_map/place_update/pallas_call | solution.py:415

commit v6 on v4

--- a/solution.py
+++ b/solution.py
@@ -17,6 +17,7 @@
 F32 = jnp.float32
 BF16 = jnp.bfloat16
 CHUNKS = 4
+SHAPE_ROWS = 512
 SPOTS = 8
 SPLIT = 1
 
@@ -240,9 +241,7 @@
         if j == min(1, late[-1]):
             pl.semaphore_wait(all_in, len(in_plane))
             hand_out(early)
-    for j in late:
-        hand_out(j)
-
+    hand_out(0)
     for copy in in_copies[:2]:
         copy.wait()
 
@@ -253,6 +252,9 @@
         return carry
 
     lax.fori_loop(0, block // tile, cast_roots, 0)
+
+    for j in late[1:]:
+        hand_out(j)
 
     for copy in in_copies[2:]:
         copy.wait()
@@ -277,18 +279,18 @@
         adam_sq = lax.fori_loop(0, block // chunk_rows, second_step, adam_sq, unroll=True)
 
         def shape_step(t, acc):
-            at = pl.ds(pl.multiple_of(t * tile, tile), tile)
+            at = pl.ds(pl.multiple_of(t * SHAPE_ROWS, SHAPE_ROWS), SHAPE_ROWS)
             left = jnp.dot(lroot[at, :], gb[:, cols], preferred_element_type=F32).astype(BF16)
             both = jnp.dot(left, rroot[cols, :], preferred_element_type=F32)
             if j != early:
                 both = both + shaped[at, :]
             if j == late[-1]:
-                both = jnp.where(lax.broadcasted_iota(jnp.int32, (tile, block), 1) < real, both, 0.0)
-                acc = acc + jnp.sum((both * both).reshape(tile // 8, 8, block), axis=0)
+                both = jnp.where(lax.broadcasted_iota(jnp.int32, (SHAPE_ROWS, block), 1) < real, both, 0.0)
+                acc = acc + jnp.sum((both * both).reshape(SHAPE_ROWS // 8, 8, block), axis=0)
             shaped[at, :] = both
             return acc
 
-        shaped_sq = lax.fori_loop(0, block // tile, shape_step, shaped_sq, unroll=True)
+        shaped_sq = lax.fori_loop(0, block // SHAPE_ROWS, shape_step, shaped_sq, unroll=True)
 
     adam_norm = jnp.sum(jnp.sum(adam_sq, axis=0, keepdims=True), axis=1, keepdims=True)
     shaped_norm = jnp.sum(jnp.sum(shaped_sq, axis=0, keepdims=True), axis=1, keepdims=True)
@@ -297,30 +299,27 @@
     per = chunk_rows // 8
     turns = shards // per
 
-    def moment_step(k, carry):
-        far = lax.div(k + 1, 2)
-        t = lax.rem(lax.div(s, per) + turns // 2 + far * (1 - 2 * lax.rem(k, 2)), turns)
+    def send_back(d):
+        pltpu.make_async_remote_copy(
+            src_ref=back.at[d],
+            dst_ref=back_arrived.at[s],
+            send_sem=b_send,
+            recv_sem=b_recv,
+            device_id=(r, d),
+            device_id_type=MESH,
+        ).start()
+
+    for k in range(turns):
+        far = (k + 1) // 2
+        t = lax.rem(lax.div(s, per) + turns // 2 + (-far if k % 2 else far), turns)
         at = pl.ds(pl.multiple_of(t * chunk_rows, chunk_rows), chunk_rows)
         moment = BETA_MOMENT * mom[at, :] + scale * shaped[at, :]
         mom[at, :] = moment
         back[pl.ds(pl.multiple_of(t * per, per), per)] = (-LEARN_RATE * moment).reshape(per, 8, block).astype(BF16)
-        for i in range(per):
-            d = t * per + i
-
-            @pl.when(d != s)
-            def _():
-                pltpu.make_async_remote_copy(
-                    src_ref=back.at[d],
-                    dst_ref=back_arrived.at[s],
-                    send_sem=b_send,
-                    recv_sem=b_recv,
-                    device_id=(r, d),
-                    device_id_type=MESH,
-                ).start()
-
-        return carry
-
-    lax.fori_loop(0, turns, moment_step, 0, unroll=True)
+        last = k == turns - 1
+        for i in range(per - 1 if last else per):
+            send_back(t * per + (lax.rem(s + 1 + i, per) if last else i))
+
     back_arrived[s] = back[s]
 
     def left_step(t, carry):

time: 53.5 us -> 53.3 us (level)
  no operation moved by 1% of the time
where the time goes in v6:
time: 53.3 us; the launch traced here: 53.2 us
  Pallas kernels  52.5 us (98%)
  between operations  0.64 us (1%)
    pallas_call x1, Pallas kernels, per_device(): pl.pallas_call(functools.partial(kernel, cfg), name='shampoo_step', out_s...  50.3 us
    pallas_call x1, Pallas kernels, per_device(): pl.pallas_call(functools.partial(finish, quarter, block), name='place_upd...  2.2 us

profile of v6, /device:TPU:1, one launch (start us, length us, event | category | flops | bytes accessed | tf_op | source)
XLA Modules:
  0.0 53.2 jit_solution(13833129809154549811)
XLA Ops:
  0.6 50.3 %shampoo_step.1 = (bf16[64,8,512]{2,1,0:T(8,128)(2,1)S(1)}, f32[512,512]{1,0:T(8,128)S(1)}, f32[512,512]{1,0:T(8,128)S(1)}, f32[512,512]{1,0:T(8,128)S(1)}, f32[512,512]{1,0:T(8,128)S(1)}) custom-call(s32[4,64]{1,0:T(4,128)} %table_in.3, bf16[32,8,3584]{2,1,0:T(8,128)(2,1)} %bitcast.11, f32[512,512]{1,0:T(8,128)} %bitcast.12, f32[512,512]{1,0:T(8,128)} %bitcast.13, ...), custom_call_target="tpu_custom_call" | custom-call | flops 1073741824 | bytes 16777216 | tf_op jit(solution)/shard_map/shampoo_step/pallas_call | solution.py:397
  51.0 2.2 %place_update.1 = (bf16[32,8,896]{2,1,0:T(8,128)(2,1)}, f32[512,512]{1,0:T(8,128)}, f32[512,512]{1,0:T(8,128)}, f32[512,512]{1,0:T(8,128)}, f32[512,512]{1,0:T(8,128)}) custom-call(s32[4,64]{1,0:T(4,128)} %table_in.3, bf16[64,8,512]{2,1,0:T(8,128)(2,1)S(1)} %get-tuple-element.15.arrived, f32[512,512]{1,0:T(8,128)S(1)} %get-tuple-element.16.mom, ...), custom_call_target="tpu_custom_call" | custom-call | tf_op jit(solution)/shard_map/place_update/pallas_call | solution.py:415
